TPU v7x, 32 devices: a whole 2x2x4 slice. The times are simulated.
32 devices in a mesh: node: 4 (over y, x), batch: 8 (over z, core).
Axes of the slice: x: 2, y: 2, z: 4, core: 2. Of those that a mesh axis runs over, the one named last changes fastest.
Arguments:
- inputs: bfloat16 [8, 6, 64, 2048], P('batch', None, None, 'node'), may hold values from -6 to 6
- w_conv: bfloat16 [128, 128], replicated, may hold values from -0.5 to 0.5
- b_conv: float32 [128], replicated, may hold values from -3 to 3
- w_mix: bfloat16 [64, 320], replicated, may hold values from -0.3125 to 0.3125
- b_mix: float32 [64], replicated, may hold values from -3 to 3
- w_skip: bfloat16 [256, 64], replicated, may hold values from -0.75 to 0.75
- b_skip: float32 [256], replicated, may hold values from -3 to 3
- local_fwd: bfloat16 [2048, 384], P('node'), may hold values from -0.25 to 0.25
- local_bwd: bfloat16 [2048, 384], P('node'), may hold values from -0.25 to 0.25
- remote_fwd: bfloat16 [16, 128, 128], P('node'), may hold values from -0.25 to 0.25
- remote_bwd: bfloat16 [16, 128, 128], P('node'), may hold values from -0.25 to 0.25
- tile_src: int32 [16], P('node'), may hold values from 0 to 3, as said below
- tile_dst: int32 [16], P('node'), may hold values from -1 to 3, as said below
- residual_cotangent: bfloat16 [8, 4, 64, 2048], P('batch', None, None, 'node'), may hold values from -6 to 6
- cot_skip: bfloat16 [8, 256, 2048], P('batch', None, 'node'), may hold values from -6 to 6
Outputs:
- residual_out: bfloat16 [8, 4, 64, 2048], P('batch', None, None, 'node')
- skip_out: bfloat16 [8, 256, 2048], P('batch', None, 'node')
- grad_x: bfloat16 [8, 6, 64, 2048], P('batch', None, None, 'node')
- grad_w_conv: float32 [128, 128], replicated
- grad_b_conv: float32 [128], replicated
- grad_w_mix: float32 [64, 320], replicated
- grad_b_mix: float32 [64], replicated
- grad_w_skip: float32 [256, 64], replicated
- grad_b_skip: float32 [256], replicated
Inputs may be any that keep to these rules, and one draw needn't show every extreme that they name: `tile_src`: entry p * 4 + q is a block of device p. `tile_dst`: entry p * 4 + q is a block of device q, or -1 where device p holds no tile for device q, always -1 for q = p.
All inputs are finite; a program needn't handle non-finite values.
Results may differ from a plain program's by a relative error of at most 0.012.
Values may be sent and summed in bfloat16 or wider, within the bound.
A program may use at most 128 MiB of HBM per device.

v0:
```python
import math

import jax
import jax.numpy as jnp
from jax import lax
from jax.sharding import PartitionSpec as P

DILATION_GAP = 2


def neighbor_stack(values, blocks, tile_width):
    row_count = values.shape[0]
    shaped = values.reshape(row_count, blocks, tile_width)
    zeros_blk = jnp.zeros((row_count, 1, tile_width), values.dtype)
    before = jnp.concatenate([zeros_blk, shaped[:, :-1]], axis=1)
    after_blk = jnp.concatenate([shaped[:, 1:], zeros_blk], axis=1)
    return jnp.concatenate([before, shaped, after_blk], axis=2)


def band_apply(values, weights):
    tile_width = weights.shape[1] // 3
    blocks = weights.shape[0] // tile_width
    stacked = neighbor_stack(values, blocks, tile_width)
    shaped_w = weights.reshape(blocks, tile_width, 3 * tile_width)
    result = jnp.einsum("mik,iak->mia", stacked, shaped_w, preferred_element_type=jnp.float32)
    return result.reshape(values.shape[0], blocks * tile_width)


def band_transpose(gradient, weights):
    tile_width = weights.shape[1] // 3
    blocks = weights.shape[0] // tile_width
    row_count = gradient.shape[0]
    shaped_w = weights.reshape(blocks, tile_width, 3 * tile_width)
    spread = jnp.einsum(
        "mia,iak->mik",
        gradient.reshape(row_count, blocks, tile_width),
        shaped_w,
        preferred_element_type=jnp.float32,
    )
    spread = spread.reshape(row_count, blocks, 3, tile_width)
    zeros_blk = jnp.zeros((row_count, 1, tile_width), jnp.float32)
    from_after = jnp.concatenate([spread[:, 1:, 0], zeros_blk], axis=1)
    from_before = jnp.concatenate([zeros_blk, spread[:, :-1, 2]], axis=1)
    return (spread[:, :, 1] + from_after + from_before).reshape(row_count, blocks * tile_width)


def pick_blocks(values, chooser):
    blocks = chooser.shape[1]
    shaped = values.reshape(values.shape[0], blocks, values.shape[1] // blocks)
    return jnp.einsum("qi,mic->qmc", chooser, shaped, preferred_element_type=jnp.float32).astype(
        jnp.bfloat16
    )


def place_blocks(pieces, chooser):
    result = jnp.einsum("qi,qmc->mic", chooser, pieces, preferred_element_type=jnp.float32)
    return result.reshape(result.shape[0], result.shape[1] * result.shape[2])


def tile_forward(pieces, tile_vals):
    return jnp.einsum("qmc,qac->qma", pieces, tile_vals, preferred_element_type=jnp.float32).astype(
        jnp.bfloat16
    )


def tile_backward(pieces, tile_vals):
    return jnp.einsum("qma,qac->qmc", pieces, tile_vals, preferred_element_type=jnp.float32)


def shards(
    inputs,
    w_conv,
    b_conv,
    w_mix,
    b_mix,
    w_skip,
    b_skip,
    local_fwd,
    local_bwd,
    remote_fwd,
    remote_bwd,
    tile_src,
    tile_dst,
    residual_cotangent,
    cot_skip,
):
    windows, input_steps, channel_count, local_nodes = inputs.shape
    output_steps = input_steps - DILATION_GAP
    tile_width = remote_fwd.shape[1]
    blocks = local_nodes // tile_width
    block_ids = jnp.arange(blocks, dtype=jnp.int32)
    own_src = (tile_src[:, None] == block_ids[None, :]).astype(jnp.bfloat16)
    own_dst = (tile_dst[:, None] == block_ids[None, :]).astype(jnp.bfloat16)
    row_count = windows * output_steps * channel_count
    shape4 = (windows, output_steps, channel_count, local_nodes)
    paired_taps = jnp.concatenate([inputs[:, :output_steps], inputs[:, DILATION_GAP:]], axis=2)
    pre_act = (
        jnp.einsum("oc,wtcn->wton", w_conv, paired_taps, preferred_element_type=jnp.float32)
        + b_conv[None, None, :, None]
    )
    filtered = jnp.tanh(pre_act[:, :, :channel_count])
    gate_val = jax.nn.sigmoid(pre_act[:, :, channel_count:])
    hidden = (filtered * gate_val).astype(jnp.bfloat16)
    flat_hidden = hidden.reshape(row_count, local_nodes)

    def push_hop(picked_fwd, picked_bwd):
        part_fwd = tile_forward(picked_fwd, remote_fwd)
        part_bwd = tile_forward(picked_bwd, remote_bwd)
        got_fwd, got_bwd, got_dst = (
            lax.all_to_all(part_fwd, "node", split_axis=0, concat_axis=0, tiled=True),
            lax.all_to_all(part_bwd, "node", split_axis=0, concat_axis=0, tiled=True),
            lax.all_to_all(own_dst, "node", split_axis=0, concat_axis=0, tiled=True),
        )
        return (place_blocks(got_fwd, got_dst), place_blocks(got_bwd, got_dst), got_dst)

    picked = pick_blocks(flat_hidden, own_src)
    far_fwd, far_bwd, recv_dst = push_hop(picked, picked)
    hop_fwd = (band_apply(flat_hidden, local_fwd) + far_fwd).astype(jnp.bfloat16)
    hop_bwd = (band_apply(flat_hidden, local_bwd) + far_bwd).astype(jnp.bfloat16)
    far_fwd, far_bwd, recv_dst = push_hop(
        pick_blocks(hop_fwd, own_src), pick_blocks(hop_bwd, own_src)
    )
    two_fwd = (band_apply(hop_fwd, local_fwd) + far_fwd).astype(jnp.bfloat16)
    two_bwd = (band_apply(hop_bwd, local_bwd) + far_bwd).astype(jnp.bfloat16)
    stacked_parts = jnp.concatenate(
        [
            hidden,
            hop_fwd.reshape(shape4),
            two_fwd.reshape(shape4),
            hop_bwd.reshape(shape4),
            two_bwd.reshape(shape4),
        ],
        axis=2,
    )
    mixed_features = (
        jnp.einsum("oc,wtcn->wton", w_mix, stacked_parts, preferred_element_type=jnp.float32)
        + b_mix[None, None, :, None]
    )
    residual_stream = (inputs[:, DILATION_GAP:].astype(jnp.float32) + mixed_features).astype(
        jnp.bfloat16
    )
    last_step = hidden[:, output_steps - 1]
    skip_sum = (
        jnp.einsum("sc,wcn->wsn", w_skip, last_step, preferred_element_type=jnp.float32)
        + b_skip[None, :, None]
    ).astype(jnp.bfloat16)
    grad_parts = jnp.einsum(
        "co,wtcn->wton", w_mix, residual_cotangent, preferred_element_type=jnp.float32
    )
    grad_mix = jnp.einsum(
        "wtcn,wton->co", residual_cotangent, stacked_parts, preferred_element_type=jnp.float32
    )
    grad_bmix = jnp.sum(residual_cotangent.astype(jnp.float32), axis=(0, 1, 3))
    grad_skip = jnp.einsum("wsn,wcn->sc", cot_skip, last_step, preferred_element_type=jnp.float32)
    grad_bskip = jnp.sum(cot_skip.astype(jnp.float32), axis=(0, 2))

    def group_of(index):
        return grad_parts[:, :, index * channel_count : (index + 1) * channel_count].reshape(
            row_count, local_nodes
        )

    back2_fwd = group_of(2).astype(jnp.bfloat16)
    back2_bwd = group_of(4).astype(jnp.bfloat16)

    def fetch_rows(grad_fwd, grad_bwd):
        return (
            lax.all_to_all(
                pick_blocks(grad_fwd, recv_dst), "node", split_axis=0, concat_axis=0, tiled=True
            ),
            lax.all_to_all(
                pick_blocks(grad_bwd, recv_dst), "node", split_axis=0, concat_axis=0, tiled=True
            ),
        )

    got_fwd, got_bwd = fetch_rows(back2_fwd, back2_bwd)
    near1_fwd = place_blocks(tile_backward(got_fwd, remote_fwd).astype(jnp.bfloat16), own_src)
    near1_bwd = place_blocks(tile_backward(got_bwd, remote_bwd).astype(jnp.bfloat16), own_src)
    back1_fwd = (group_of(1) + band_transpose(back2_fwd, local_fwd) + near1_fwd).astype(
        jnp.bfloat16
    )
    back1_bwd = (group_of(3) + band_transpose(back2_bwd, local_bwd) + near1_bwd).astype(
        jnp.bfloat16
    )
    got_fwd, got_bwd = fetch_rows(back1_fwd, back1_bwd)
    combined = (tile_backward(got_fwd, remote_fwd) + tile_backward(got_bwd, remote_bwd)).astype(
        jnp.bfloat16
    )
    far_total = place_blocks(combined, own_src)
    skip_back = jnp.einsum("sc,wsn->wcn", w_skip, cot_skip, preferred_element_type=jnp.float32)
    direct = (
        grad_parts[:, :, :channel_count]
        .at[:, output_steps - 1]
        .add(skip_back)
        .reshape(row_count, local_nodes)
    )
    summed = (
        direct
        + band_transpose(back1_fwd, local_fwd)
        + band_transpose(back1_bwd, local_bwd)
        + far_total
    )
    grad_hidden = summed.astype(jnp.bfloat16).reshape(shape4).astype(jnp.float32)
    grad_pre = jnp.concatenate(
        [
            grad_hidden * gate_val * (1.0 - filtered * filtered),
            grad_hidden * filtered * gate_val * (1.0 - gate_val),
        ],
        axis=2,
    ).astype(jnp.bfloat16)
    tap_gradients = jnp.einsum(
        "oc,wton->wtcn", w_conv, grad_pre, preferred_element_type=jnp.float32
    )
    input_gradient = jnp.zeros((windows, input_steps, channel_count, local_nodes), jnp.float32)
    input_gradient = input_gradient.at[:, :output_steps].add(tap_gradients[:, :, :channel_count])
    input_gradient = input_gradient.at[:, DILATION_GAP:].add(
        tap_gradients[:, :, channel_count:] + residual_cotangent.astype(jnp.float32)
    )
    grad_wconv = jnp.einsum(
        "wton,wtcn->oc", grad_pre, paired_taps, preferred_element_type=jnp.float32
    )
    grad_bconv = jnp.sum(grad_pre.astype(jnp.float32), axis=(0, 1, 3))
    totals = lax.psum(
        (grad_wconv, grad_bconv, grad_mix, grad_bmix, grad_skip, grad_bskip), ("node", "batch")
    )
    grad_count = (
        windows * lax.axis_size("batch") * local_nodes * lax.axis_size("node") * output_steps
    )
    grad_scale = 1.0 / math.sqrt(float(grad_count))
    return (
        residual_stream,
        skip_sum,
        input_gradient.astype(jnp.bfloat16),
        totals[0] * grad_scale,
        totals[1] * grad_scale,
        totals[2] * grad_scale,
        totals[3] * grad_scale,
        totals[4] * grad_scale,
        totals[5] * grad_scale,
    )


def solution(mesh):
    return jax.shard_map(
        shards,
        mesh=mesh,
        in_specs=(
            P("batch", None, None, "node"),
            P(),
            P(),
            P(),
            P(),
            P(),
            P(),
            P("node", None),
            P("node", None),
            P("node", None, None),
            P("node", None, None),
            P("node"),
            P("node"),
            P("batch", None, None, "node"),
            P("batch", None, "node"),
        ),
        out_specs=(
            P("batch", None, None, "node"),
            P("batch", None, "node"),
            P("batch", None, None, "node"),
            P(),
            P(),
            P(),
            P(),
            P(),
            P(),
        ),
        check_vma=False,
    )
```

profile of v0, /device:TPU:0, one launch (start us, length us, event | category | flops | bytes accessed | tf_op | source)
XLA Modules:
  0.0 353.8 jit_solution(16946161396130707570)
XLA Ops:
  7.2 1.4 compare_convert_fusion
  8.5 5.2 %all-to-all-start.1 = ((bf16[4,1,4]{2,1,0:T(2,128)(2,1)}), bf16[4,1,4]{2,1,0:T(2,128)(2,1)S(1)}, u32[]{:S(2)}, u32[]{:S(2)}) async-start(bf16[4,1,4]{2,1,0:T(2,128)(2,1)} %compare_convert_fusion), calls=%async_computation.1 | async-start | bytes 4096 | tf_op jit(solution)/shard_map/all_to_all | solution.py:112
  13.7 1.5 convolution_bitcast_fusion
  17.2 2.6 convolution_bitcast_fusion.4
  19.8 3.1 copy.249
  22.8 2.1 fusion.154
  24.9 1.9 slice.221
  26.8 1.2 fusion.151
  34.2 2.0 copy.298
  36.2 2.0 copy.299
  38.2 2.0 copy.297
  40.2 2.0 reshape.437
  42.2 2.0 copy.303
  44.3 2.0 copy.304
  46.3 2.0 copy.302
  48.3 2.0 reshape.441
  53.5 1.8 fusion.44
  57.2 4.2 %all-to-all-start.3 = ((bf16[4,256,128]{2,1,0:T(8,128)(2,1)}), bf16[4,256,128]{2,1,0:T(8,128)(2,1)}, u32[]{:S(2)}, u32[]{:S(2)}) async-start(bf16[4,256,128]{2,1,0:T(8,128)(2,1)} %convolution_convert_fusion.7), calls=%async_computation.3 | async-start | bytes 524288 | tf_op jit(solution)/shard_map/all_to_all | solution.py:111
  63.5 3.4 all-to-all-done.3
  66.9 4.0 %all-to-all-start = ((bf16[4,256,128]{2,1,0:T(8,128)(2,1)}), bf16[4,256,128]{2,1,0:T(8,128)(2,1)}, u32[]{:S(2)}, u32[]{:S(2)}) async-start(bf16[4,256,128]{2,1,0:T(8,128)(2,1)} %convolution_convert_fusion.9), calls=%async_computation | async-start | bytes 524288 | tf_op jit(solution)/shard_map/all_to_all | solution.py:110
  70.9 1.3 fusion.102
  73.3 1.6 fusion.39
  76.4 4.0 %all-to-all-start.6 = ((bf16[4,256,128]{2,1,0:T(8,128)(2,1)}), bf16[4,256,128]{2,1,0:T(8,128)(2,1)}, u32[]{:S(2)}, u32[]{:S(2)}) async-start(bf16[4,256,128]{2,1,0:T(8,128)(2,1)} %copy.265), calls=%async_computation.6 | async-start | bytes 524288 | tf_op jit(solution)/shard_map/all_to_all | solution.py:170
  80.4 1.3 fusion.107
  82.7 2.5 fusion.37
  85.3 1.2 copy.226
  90.4 1.9 convolution_convert_fusion.8
  94.1 4.1 %all-to-all-start.5 = ((bf16[4,256,128]{2,1,0:T(8,128)(2,1)}), bf16[4,256,128]{2,1,0:T(8,128)(2,1)}, u32[]{:S(2)}, u32[]{:S(2)}) async-start(bf16[4,256,128]{2,1,0:T(8,128)(2,1)} %copy.253), calls=%async_computation.5 | async-start | bytes 524288 | tf_op jit(solution)/shard_map/all_to_all | solution.py:167
  98.3 1.2 convolution_convert_fusion.2
  99.5 1.9 fusion.36
  101.3 1.5 convolution_bitcast_fusion.1
  103.8 4.2 %all-to-all-start.4 = ((bf16[4,256,128]{2,1,0:T(8,128)(2,1)}), bf16[4,256,128]{2,1,0:T(8,128)(2,1)}, u32[]{:S(2)}, u32[]{:S(2)}) async-start(bf16[4,256,128]{2,1,0:T(8,128)(2,1)} %convolution_convert_fusion.6), calls=%async_computation.4 | async-start | bytes 524288 | tf_op jit(solution)/shard_map/all_to_all | solution.py:111
  108.1 1.2 convolution_convert_fusion.4
  109.3 2.0 fusion.35
  111.4 1.6 convolution_bitcast_fusion.3
  113.0 3.0 copy.256
  116.0 1.2 slice_bitcast_fusion.5
  117.2 1.9 fusion.78
  119.1 2.0 copy.259
  121.1 2.0 reshape.440
  123.2 3.0 copy.268
  126.2 1.2 slice_bitcast_fusion.3
  127.4 1.9 fusion.76
  129.3 2.0 copy.271
  131.4 2.1 reshape.444
  133.4 1.7 copy.273
  136.2 4.2 %all-to-all-start.2 = ((bf16[4,256,128]{2,1,0:T(8,128)(2,1)}), bf16[4,256,128]{2,1,0:T(8,128)(2,1)}, u32[]{:S(2)}, u32[]{:S(2)}) async-start(bf16[4,256,128]{2,1,0:T(8,128)(2,1)} %convolution_convert_fusion.8), calls=%async_computation.2 | async-start | bytes 524288 | tf_op jit(solution)/shard_map/all_to_all | solution.py:110
  140.4 1.3 fusion.99
  141.7 1.4 fusion.40
  144.2 1.7 all-to-all-done.2
  145.9 3.4 all-to-all-start.7
  149.3 1.3 fusion.104
  150.6 1.6 fusion.38
  156.2 2.0 fusion.31
  159.4 4.2 %all-to-all-start.8 = ((bf16[4,256,128]{2,1,0:T(8,128)(2,1)}), bf16[4,256,128]{2,1,0:T(8,128)(2,1)S(1)}, u32[]{:S(2)}, u32[]{:S(2)}) async-start(bf16[4,256,128]{2,1,0:T(8,128)(2,1)} %copy.273), calls=%async_computation.8 | async-start | bytes 524288 | tf_op jit(solution)/shard_map/all_to_all | solution.py:170
  164.6 4.3 %all-to-all-done.8 = bf16[4,256,128]{2,1,0:T(8,128)(2,1)S(1)} async-done(((bf16[4,256,128]{2,1,0:T(8,128)(2,1)}), bf16[4,256,128]{2,1,0:T(8,128)(2,1)S(1)}, u32[]{:S(2)}, u32[]{:S(2)}) %all-to-all-start.8) | async-done | bytes 262176 | tf_op jit(solution)/shard_map/all_to_all | solution.py:170
  169.0 1.3 fusion.41
  171.3 1.3 reshape.445
  172.6 1.4 fusion.69
  176.8 39.6 %all-reduce.15 = (f32[128]{0:T(128)S(1)}, f32[64]{0:T(128)S(1)}, f32[256]{0:T(256)S(1)}) all-reduce(f32[128]{0:T(128)S(1)} %convert_reduce_fusion, f32[64]{0:T(128)S(1)} %get-tuple-element.115, f32[256]{0:T(256)S(1)} %convert_reduce_fusion.2), channel_id=1, replica_groups=mesh['node'=4,'batch'=8] {'node','batch'}, use_global_device_ids=true, to_apply=%region_2.0 | all-reduce | flops 448 | bytes 3584 | tf_op jit(solution)/shard_map/psum | solution.py:222
  218.8 123.6 %all-reduce.19.cloned.1.call-done = (f32[128,128]{1,0:T(8,128)}, f32[64,320]{1,0:T(8,128)}, f32[256,64]{0,1:T(8,128)}) async-done(((f32[128,128]{1,0:T(8,128)}, f32[64,320]{1,0:T(8,128)}, f32[256,64]{0,1:T(8,128)}), (f32[128,128]{1,0:T(8,128)}, f32[64,320]{1,0:T(8,128)}, f32[256,64]{0,1:T(8,128)})) %all-reduce.19.cloned.1.call-update) | async-done | bytes 213008 | tf_op jit(solution)/shard_map/psum | solution.py:222
  342.5 1.5 broadcast_multiply_fusion
  344.0 1.5 broadcast_multiply_fusion.1
  345.5 1.5 broadcast_multiply_fusion.2
  (140 shorter events, 39.8 us)
Async XLA Ops:
  7.2 20.9 %copy-start = (bf16[512,384]{1,0:T(8,128)(2,1)S(1)}, bf16[512,384]{1,0:T(8,128)(2,1)}, u32[]{:S(2)}) copy-start(bf16[512,384]{1,0:T(8,128)(2,1)} %param.29) | copy-start | bytes 1179652
  8.5 48.7 %all-to-all-start.1 = ((bf16[4,1,4]{2,1,0:T(2,128)(2,1)}), bf16[4,1,4]{2,1,0:T(2,128)(2,1)S(1)}, u32[]{:S(2)}, u32[]{:S(2)}) async-start(bf16[4,1,4]{2,1,0:T(2,128)(2,1)} %compare_convert_fusion), calls=%async_computation.1 | async-start | bytes 4096 | tf_op jit(solution)/shard_map/all_to_all | solution.py:112
  15.2 11.6 %copy-start.1 = (f32[1,4,320,512]{3,2,1,0:T(8,128)}, f32[1,4,320,512]{3,2,1,0:T(8,128)S(1)}, u32[]{:S(2)}) copy-start(f32[1,4,320,512]{3,2,1,0:T(8,128)S(1)} %convolution_bitcast_fusion) | copy-start | bytes 7864324
  17.2 5.6 %copy-start.3 = (bf16[256,4,128]{2,1,0:T(4,128)(2,1)}, bf16[256,4,128]{2,1,0:T(4,128)(2,1)S(1)}, u32[]{:S(2)}) copy-start(bf16[256,4,128]{2,1,0:T(4,128)(2,1)S(1)} %convert_element_type.211) | copy-start | bytes 786436
  28.1 0.7 copy-start.5
  29.6 1.8 copy-start.22
  29.6 2.7 copy-start.29
  29.6 2.7 copy-start.34
  31.5 0.7 copy-start.24
  31.5 0.8 copy-start.26
  32.3 1.0 copy-start.7
  32.8 7.4 %copy-start.21 = (bf16[1,4,64,512]{3,2,1,0:T(8,128)(2,1)}, bf16[1,4,64,512]{3,2,1,0:T(8,128)(2,1)S(1)}, u32[]{:S(2)}) copy-start(bf16[1,4,64,512]{3,2,1,0:T(8,128)(2,1)S(1)} %get-tuple-element.99) | copy-start | bytes 786436
  44.2 6.2 %copy-start.32 = (s32[4]{0:T(128)S(1)}, s32[4]{0:T(128)}, u32[]{:S(2)}) copy-start(s32[4]{0:T(128)} %param.32) | copy-start | bytes 52
  48.3 3.3 copy-start.10
  48.3 4.2 %copy-start.8 = (bf16[4,128,128]{2,1,0:T(8,128)(2,1)S(1)}, bf16[4,128,128]{2,1,0:T(8,128)(2,1)}, u32[]{:S(2)}) copy-start(bf16[4,128,128]{2,1,0:T(8,128)(2,1)} %param.30) | copy-start | bytes 393220
  50.4 3.1 copy-start.31
  50.4 4.9 %copy-start.19 = (bf16[256,4,128]{2,0,1:T(8,128)(2,1)}, bf16[256,4,128]{2,0,1:T(8,128)(2,1)S(1)}, u32[]{:S(2)}) copy-start(bf16[256,4,128]{2,0,1:T(8,128)(2,1)S(1)} %copy.218) | copy-start | bytes 786436
  50.4 4.8 %copy-start.33 = (f32[256]{0:T(256)S(1)}, f32[256]{0:T(256)}, u32[]{:S(2)}) copy-start(f32[256]{0:T(256)} %param.27) | copy-start | bytes 3076
  51.6 9.8 %copy-start.4 = (bf16[256,4,128]{2,1,0:T(4,128)(2,1)S(1)}, bf16[256,4,128]{2,1,0:T(4,128)(2,1)}, u32[]{:S(2)}) copy-start(bf16[256,4,128]{2,1,0:T(4,128)(2,1)} %copy-done.3) | copy-start | bytes 786436
  53.5 9.0 %copy-start.6 = (bf16[256,4,128]{2,1,0:T(4,128)(2,1)S(1)}, bf16[256,4,128]{2,1,0:T(4,128)(2,1)}, u32[]{:S(2)}) copy-start(bf16[256,4,128]{2,1,0:T(4,128)(2,1)} %copy-done.5) | copy-start | bytes 786436
  57.2 9.7 %all-to-all-start.3 = ((bf16[4,256,128]{2,1,0:T(8,128)(2,1)}), bf16[4,256,128]{2,1,0:T(8,128)(2,1)}, u32[]{:S(2)}, u32[]{:S(2)}) async-start(bf16[4,256,128]{2,1,0:T(8,128)(2,1)} %convolution_convert_fusion.7), calls=%async_computation.3 | async-start | bytes 524288 | tf_op jit(solution)/shard_map/all_to_all | solution.py:111
  62.7 10.5 %copy-start.20 = (bf16[256,4,128]{2,0,1:T(8,128)(2,1)S(1)}, bf16[256,4,128]{2,0,1:T(8,128)(2,1)}, u32[]{:S(2)}) copy-start(bf16[256,4,128]{2,0,1:T(8,128)(2,1)} %copy-done.19) | copy-start | bytes 786436
  66.9 9.5 %all-to-all-start = ((bf16[4,256,128]{2,1,0:T(8,128)(2,1)}), bf16[4,256,128]{2,1,0:T(8,128)(2,1)}, u32[]{:S(2)}, u32[]{:S(2)}) async-start(bf16[4,256,128]{2,1,0:T(8,128)(2,1)} %convolution_convert_fusion.9), calls=%async_computation | async-start | bytes 524288 | tf_op jit(solution)/shard_map/all_to_all | solution.py:110
  74.9 1.5 copy-start.17
  76.4 17.8 %all-to-all-start.6 = ((bf16[4,256,128]{2,1,0:T(8,128)(2,1)}), bf16[4,256,128]{2,1,0:T(8,128)(2,1)}, u32[]{:S(2)}, u32[]{:S(2)}) async-start(bf16[4,256,128]{2,1,0:T(8,128)(2,1)} %copy.265), calls=%async_computation.6 | async-start | bytes 524288 | tf_op jit(solution)/shard_map/all_to_all | solution.py:170
  85.3 4.2 %copy-start.11 = (bf16[4,128,128]{2,1,0:T(8,128)(2,1)S(1)}, bf16[4,128,128]{2,1,0:T(8,128)(2,1)}, u32[]{:S(2)}) copy-start(bf16[4,128,128]{2,1,0:T(8,128)(2,1)} %param.31) | copy-start | bytes 393220
  85.3 5.1 %copy-start.9 = (bf16[4,128,128]{2,1,0:T(8,128)(2,1)S(1)}, bf16[4,128,128]{2,1,0:T(8,128)(2,1)}, u32[]{:S(2)}) copy-start(bf16[4,128,128]{2,1,0:T(8,128)(2,1)} %param.30) | copy-start | bytes 393220
  89.5 3.9 %copy-start.15 = (bf16[256,4,128]{0,2,1:T(8,128)(2,1)S(1)}, bf16[256,4,128]{0,2,1:T(8,128)(2,1)}, u32[]{:S(2)}) copy-start(bf16[256,4,128]{0,2,1:T(8,128)(2,1)} %fusion.37) | copy-start | bytes 786436
  90.4 9.0 %copy-start.14 = (f32[256,3,1,128]{3,1,0,2:T(4,128)S(1)}, f32[256,3,1,128]{3,1,0,2:T(4,128)}, u32[]{:S(2)}) copy-start(f32[256,3,1,128]{3,1,0,2:T(4,128)} %copy.303) | copy-start | bytes 1179652
  94.1 9.7 %all-to-all-start.5 = ((bf16[4,256,128]{2,1,0:T(8,128)(2,1)}), bf16[4,256,128]{2,1,0:T(8,128)(2,1)}, u32[]{:S(2)}, u32[]{:S(2)}) async-start(bf16[4,256,128]{2,1,0:T(8,128)(2,1)} %copy.253), calls=%async_computation.5 | async-start | bytes 524288 | tf_op jit(solution)/shard_map/all_to_all | solution.py:167
  103.8 32.3 %all-to-all-start.4 = ((bf16[4,256,128]{2,1,0:T(8,128)(2,1)}), bf16[4,256,128]{2,1,0:T(8,128)(2,1)}, u32[]{:S(2)}, u32[]{:S(2)}) async-start(bf16[4,256,128]{2,1,0:T(8,128)(2,1)} %convolution_convert_fusion.6), calls=%async_computation.4 | async-start | bytes 524288 | tf_op jit(solution)/shard_map/all_to_all | solution.py:111
  108.1 3.3 copy-start.23
  133.4 8.3 %copy-start.18 = (bf16[256,4,128]{0,2,1:T(8,128)(2,1)S(1)}, bf16[256,4,128]{0,2,1:T(8,128)(2,1)}, u32[]{:S(2)}) copy-start(bf16[256,4,128]{0,2,1:T(8,128)(2,1)} %copy-done.17) | copy-start | bytes 786436
  136.2 9.7 %all-to-all-start.2 = ((bf16[4,256,128]{2,1,0:T(8,128)(2,1)}), bf16[4,256,128]{2,1,0:T(8,128)(2,1)}, u32[]{:S(2)}, u32[]{:S(2)}) async-start(bf16[4,256,128]{2,1,0:T(8,128)(2,1)} %convolution_convert_fusion.8), calls=%async_computation.2 | async-start | bytes 524288 | tf_op jit(solution)/shard_map/all_to_all | solution.py:110
  143.1 7.4 %copy-start.16 = (bf16[256,4,128]{0,2,1:T(8,128)(2,1)S(1)}, bf16[256,4,128]{0,2,1:T(8,128)(2,1)}, u32[]{:S(2)}) copy-start(bf16[256,4,128]{0,2,1:T(8,128)(2,1)} %fusion.37) | copy-start | bytes 786436
  145.9 13.6 %all-to-all-start.7 = ((bf16[4,256,128]{2,1,0:T(8,128)(2,1)}), bf16[4,256,128]{2,1,0:T(8,128)(2,1)S(1)}, u32[]{:S(2)}, u32[]{:S(2)}) async-start(bf16[4,256,128]{2,1,0:T(8,128)(2,1)} %copy.272), calls=%async_computation.7 | async-start | bytes 524288 | tf_op jit(solution)/shard_map/all_to_all | solution.py:167
  152.2 4.0 %copy-start.35 = (f32[64]{0:T(128)S(1)}, f32[64]{0:T(128)}, u32[]{:S(2)}) copy-start(f32[64]{0:T(128)} %param.25) | copy-start | bytes 772
  154.2 2.1 copy-start.28
  154.2 4.1 %copy-start.2 = (bf16[1,4,64,512]{3,2,1,0:T(8,128)(2,1)S(1)}, bf16[1,4,64,512]{3,2,1,0:T(8,128)(2,1)}, u32[]{:S(2)}) copy-start(bf16[1,4,64,512]{3,2,1,0:T(8,128)(2,1)} %param.34) | copy-start | bytes 786436
  159.4 9.5 %all-to-all-start.8 = ((bf16[4,256,128]{2,1,0:T(8,128)(2,1)}), bf16[4,256,128]{2,1,0:T(8,128)(2,1)S(1)}, u32[]{:S(2)}, u32[]{:S(2)}) async-start(bf16[4,256,128]{2,1,0:T(8,128)(2,1)} %copy.273), calls=%async_computation.8 | async-start | bytes 524288 | tf_op jit(solution)/shard_map/all_to_all | solution.py:170
  163.6 178.9 %all-reduce.19.cloned.1.call-start = ((), (), s32[]{:S(2)}) async-start(), calls=%async_computation.9 | async-start | bytes 458752 | tf_op jit(solution)/shard_map/psum | solution.py:222
  164.6 8.0 %copy-start.12 = (f32[1,4,64,512]{3,2,1,0:T(8,128)S(1)}, f32[1,4,64,512]{3,2,1,0:T(8,128)}, u32[]{:S(2)}) copy-start(f32[1,4,64,512]{3,2,1,0:T(8,128)} %reshape.440) | copy-start | bytes 1572868
  164.6 8.0 %copy-start.13 = (f32[1,4,64,512]{3,2,1,0:T(8,128)S(1)}, f32[1,4,64,512]{3,2,1,0:T(8,128)}, u32[]{:S(2)}) copy-start(f32[1,4,64,512]{3,2,1,0:T(8,128)} %reshape.444) | copy-start | bytes 1572868
  174.0 1.0 copy-start.25
  174.0 1.0 copy-start.27
  174.3 1.7 copy-start.30
Sparse Core Ops, SparseCore 0:
  217.6 124.7 all-reduce.18
where the time goes:
time: 357 us; the launch traced here: 354 us
  waiting for transfers between devices  134 us (38%)
  local copies, waits for them, and re-layouts  67.5 us (19%)
  matrix products  46.4 us (13%)
  blocking collectives  39.6 us (11%)
  starting transfers between devices  37.6 us (11%)
  between operations  14.7 us (4%)
  other arithmetic  14.5 us (4%)
    psum x1, waiting for transfers between devices, shards(): lax.psum((grad_wconv, grad_bconv, grad_mix, grad_bmix, grad_skip, grad_bs...  124 us
    psum x1, blocking collectives, shards(): lax.psum((grad_wconv, grad_bconv, grad_mix, grad_bmix, grad_skip, grad_bs...  39.6 us
    unnamed x83, local copies, waits for them, and re-layouts  17.6 us
    dot_general x7, matrix products, place_blocks(): jnp.einsum('qi,qmc->mic', chooser, pieces, preferred_element_type=jnp.flo...  10.2 us
    transpose x4, local copies, waits for them, and re-layouts, band_transpose(): jnp.einsum('mia,iak->mik', gradient.reshape(row_count, blocks, tile_width...  9.55 us
    all_to_all x2, starting transfers between devices, push_hop(): lax.all_to_all(part_bwd, 'node', split_axis=0, concat_axis=0, tiled=True)  8.42 us
    all_to_all x2, starting transfers between devices, push_hop(): lax.all_to_all(part_fwd, 'node', split_axis=0, concat_axis=0, tiled=True)  8.23 us
    all_to_all x2, starting transfers between devices, fetch_rows(): lax.all_to_all(pick_blocks(grad_bwd, recv_dst), 'node', split_axis=0, con...  8.19 us
  transfers between devices with their start and end apart: 10, of which 5 were waited for; matrix products, arithmetic and copies ran while one was open for 32% of the time, Pallas kernels for 0%

commit v1 on v0

v1 whole, which is shorter than its diff:
```python
import functools
import math

import jax
import jax.numpy as jnp
from jax import lax
from jax.experimental import pallas as pl
from jax.experimental.pallas import tpu as pltpu
from jax.sharding import PartitionSpec as P

DILATION_GAP = 2
MESH = pl.DeviceIdType.MESH
BF16 = jnp.bfloat16
F32 = jnp.float32


def nn(a, b):
    return lax.dot_general(a, b, (((1,), (0,)), ((), ())), preferred_element_type=F32)


def nt(a, b):
    return lax.dot_general(a, b, (((1,), (1,)), ((), ())), preferred_element_type=F32)


def identity(size):
    rows = lax.broadcasted_iota(jnp.int32, (size, size), 0)
    cols = lax.broadcasted_iota(jnp.int32, (size, size), 1)
    return (rows == cols).astype(F32).astype(BF16)


def pick_mask(row, block):
    return (row == block).astype(F32)


def lanes(block, width):
    return slice(block * width, (block + 1) * width)


def kernel(
    sizes,
    x_ref, wc_ref, bc_ref, wm_ref, bm_ref, ws_ref, bs_ref, lf_ref, lb_ref, rf_ref, rb_ref,
    src_ref, dst_ref, rc_ref, cs_ref,
    res_ref, skip_ref, gx_ref, gwc_ref, gbc_ref, gwm_ref, gbm_ref, gws_ref, gbs_ref,
    dense_f, dense_b, hold_f, hold_b, far_f, far_b,
    dst_out, dst_in, tile_in,
    h_out, h_in, rc_out, rc_in, back_out, back_in, two_out, two_in,
    filt, gate, hid, pre, near_f, near_b, base0, base1, base3, mix0, mix1, mix3, hop_f, hop_b,
    one_f, one_b, u_f, u_b,
    early, early_rs, early_node, early_all, late, late_rs, late_node, late_all,
    tile_sem, node_sem, red_sem,
):
    n_node, n_batch, steps, chans, scale = sizes
    width = rf_ref.shape[1]
    blocks = lf_ref.shape[0] // width
    me = lax.axis_index("node")
    row = lax.axis_index("batch")
    offsets = range(1, n_node)
    ahead = [lax.rem(me + r, n_node) for r in offsets]
    behind = [lax.rem(me + n_node - r, n_node) for r in offsets]
    mates = [lax.rem(row + r, n_batch) for r in range(1, n_batch)]

    barrier = pltpu.get_barrier_semaphore()
    for peer in ahead:
        pl.semaphore_signal(barrier, inc=1, device_id={"node": peer}, device_id_type=MESH)
    for peer in mates:
        pl.semaphore_signal(barrier, inc=1, device_id={"batch": peer}, device_id_type=MESH)
    pl.semaphore_wait(barrier, n_node - 1 + n_batch - 1)

    started = []

    def send(src, dst, sems, at, device):
        copy = pltpu.make_async_remote_copy(
            src_ref=src, dst_ref=dst,
            send_sem=sems.at[(0, *at)], recv_sem=sems.at[(1, *at)],
            device_id=device, device_id_type=MESH,
        )
        copy.start()
        started.append(copy)
        return copy

    def step(t):
        return slice(t * chans, (t + 1) * chans)

    id_copies, tile_copies = [], []
    for k, peer in enumerate(ahead):
        dst_out[k] = jnp.full((8, 128), dst_ref[peer], jnp.int32)
        id_copies.append(send(dst_out.at[k], dst_in.at[k], node_sem, (0, k), {"node": peer}))
    for k, peer in enumerate(ahead):
        tile_copies.append(
            (
                send(rf_ref.at[peer], tile_in.at[0, k], tile_sem, (0, k), {"node": peer}),
                send(rb_ref.at[peer], tile_in.at[1, k], tile_sem, (1, k), {"node": peer}),
            )
        )
    src_rows = [jnp.full((1, width), src_ref[peer], jnp.int32) for peer in ahead]

    hid_pick = [[pick_mask(src_rows[k], j).astype(BF16) for j in range(blocks)] for k in range(n_node - 1)]
    bias = jnp.broadcast_to(bc_ref[...], (2 * chans, 2 * chans)).T
    bias = jnp.concatenate([bias] * (blocks * width // (2 * chans)), axis=1)
    taps = [
        jnp.concatenate([x_ref[step(t), :], x_ref[step(t + DILATION_GAP), :]], axis=0)
        for t in range(steps)
    ]
    for t in range(steps):
        act = nn(wc_ref[...], taps[t]) + bias
        f = jnp.tanh(act[:chans])
        s = jax.nn.sigmoid(act[chans:])
        filt[step(t), :] = f
        gate[step(t), :] = s
        hid[step(t), :] = (f * s).astype(BF16)

    h_copies = []
    for k, peer in enumerate(ahead):
        picked = hid[:, lanes(0, width)] * hid_pick[k][0]
        for j in range(1, blocks):
            picked += hid[:, lanes(j, width)] * hid_pick[k][j]
        h_out[k] = picked
        h_copies.append(send(h_out.at[k], h_in.at[k], node_sem, (1, k), {"node": peer}))

    rc_copies = []
    dst_masks = []
    for k, peer in enumerate(behind):
        id_copies[k].wait_recv()
        got = dst_in[k][0:1, :]
        dst_masks.append([pick_mask(got, i) for i in range(blocks)])
        picked = rc_ref[:, lanes(0, width)] * dst_masks[k][0].astype(BF16)
        for i in range(1, blocks):
            picked += rc_ref[:, lanes(i, width)] * dst_masks[k][i].astype(BF16)
        rc_out[k] = picked
        rc_copies.append(send(rc_out.at[k], rc_in.at[k], node_sem, (2, k), {"node": peer}))

    for dense, local in ((dense_f, lf_ref), (dense_b, lb_ref)):
        for i in range(blocks):
            for j in range(blocks):
                o = j - i + 1
                if 0 <= o <= 2:
                    dense[lanes(i, width), lanes(j, width)] = local[lanes(i, width), lanes(o, width)]
                else:
                    dense[lanes(i, width), lanes(j, width)] = jnp.zeros((width, width), BF16)
    for k, peer in enumerate(ahead):
        for hold, tiles in ((hold_f, rf_ref), (hold_b, rb_ref)):
            tile = tiles[peer]
            for j in range(blocks):
                hold[lanes(k, width), lanes(j, width)] = tile * hid_pick[k][j]

    mix_t = nt(identity(5 * chans), wm_ref[...]).astype(BF16)
    conv_t = nt(identity(2 * chans), wc_ref[...]).astype(BF16)
    skip_t = nt(identity(chans), ws_ref[...]).astype(BF16)
    mix_w = [wm_ref[:, lanes(g, chans)] for g in range(5)]

    for t in range(steps):
        cot = rc_ref[step(t), :]
        base0[step(t), :] = nn(mix_t[lanes(0, chans)], cot)
        base1[step(t), :] = nn(mix_t[lanes(1, chans)], cot)
        base3[step(t), :] = nn(mix_t[lanes(3, chans)], cot)
        h_t = hid[step(t), :]
        mix0[step(t), :] = nn(mix_w[0], h_t)
        mix1[step(t), :] = nn(mix_w[1], h_t)
        mix3[step(t), :] = nn(mix_w[3], h_t)
    last = step(steps - 1)
    base0[last, :] += nn(skip_t, cs_ref[...])
    near_f[...] = nn(rc_ref[...], dense_f[...])
    near_b[...] = nn(rc_ref[...], dense_b[...])
    hop_f32 = nt(hid[...], dense_f[...])
    hop_b32 = nt(hid[...], dense_b[...])

    skip = nn(ws_ref[...], hid[last, :])
    half = 128
    for g in range(skip.shape[0] // half):
        part = jnp.broadcast_to(bs_ref[:, lanes(g, half)], (half, half)).T
        part = jnp.concatenate([part] * (blocks * width // half), axis=1)
        skip_ref[lanes(g, half), :] = (skip[lanes(g, half), :] + part).astype(BF16)
    ones = jnp.ones((16, blocks * width), BF16)
    early[...] = jnp.zeros_like(early)
    late[...] = jnp.zeros_like(late)

    for k in range(n_node - 1):
        tile_copies[k][0].wait_recv()
        tile_copies[k][1].wait_recv()
        for i in range(blocks):
            mask = dst_masks[k][i].astype(BF16)
            far_f[lanes(i, width), lanes(k, width)] = tile_in[0, k] * mask
            far_b[lanes(i, width), lanes(k, width)] = tile_in[1, k] * mask

    for copy in h_copies:
        copy.wait_recv()
    far_h = jnp.concatenate([h_in[k] for k in range(n_node - 1)], axis=1)
    hop_f[...] = (hop_f32 + nt(far_h, far_f[...])).astype(BF16)
    hop_b[...] = (hop_b32 + nt(far_h, far_b[...])).astype(BF16)
    for t in range(steps):
        u_f[step(t), :] = (mix1[step(t), :] + nn(mix_w[2], hop_f[step(t), :])).astype(BF16)
        u_b[step(t), :] = (mix3[step(t), :] + nn(mix_w[4], hop_b[step(t), :])).astype(BF16)
    terms = nt(u_f[...], hold_f[...]) + nt(u_b[...], hold_b[...])
    two_copies = []
    for k, peer in enumerate(ahead):
        two_out[k] = terms[:, lanes(k, width)].astype(BF16)
        two_copies.append(send(two_out.at[k], two_in.at[k], node_sem, (3, k), {"node": peer}))

    for copy in rc_copies:
        copy.wait_recv()
    far_rc = jnp.concatenate([rc_in[k] for k in range(n_node - 1)], axis=1)
    r1_f = (near_f[...] + nn(far_rc, hold_f[...])).astype(BF16)
    r1_b = (near_b[...] + nn(far_rc, hold_b[...])).astype(BF16)
    for t in range(steps):
        one_f[step(t), :] = (base1[step(t), :] + nn(mix_t[lanes(2, chans)], r1_f[step(t)])).astype(BF16)
        one_b[step(t), :] = (base3[step(t), :] + nn(mix_t[lanes(4, chans)], r1_b[step(t)])).astype(BF16)
    terms = nn(one_f[...], far_f[...]) + nn(one_b[...], far_b[...])
    back_copies = []
    for k, peer in enumerate(behind):
        back_out[k] = terms[:, lanes(k, width)].astype(BF16)
        back_copies.append(send(back_out.at[k], back_in.at[k], node_sem, (4, k), {"node": peer}))

    def put(buffer, top, value):
        rows = buffer.shape[1]
        value = value.astype(BF16)
        at = top
        while at < top + value.shape[0]:
            c, o = at // rows, at % rows
            n = min(rows - o, top + value.shape[0] - at)
            buffer[c, o : o + n, 0 : value.shape[1]] = value[at - top : at - top + n]
            at += n

    def take(buffer, top, count, cols):
        rows = buffer.shape[1]
        parts = []
        at = top
        while at < top + count:
            c, o = at // rows, at % rows
            n = min(rows - o, top + count - at)
            parts.append(buffer[c, o : o + n, 0:cols].astype(F32))
            at += n
        return parts[0] if len(parts) == 1 else jnp.concatenate(parts, axis=0)

    groups = [None] * 5
    mix_bias = None

    def plus(a, b):
        return b if a is None else a + b

    for t in range(steps):
        cot = rc_ref[step(t), :]
        groups[0] = plus(groups[0], nt(cot, hid[step(t), :]))
        groups[1] = plus(groups[1], nt(cot, hop_f[step(t), :]))
        groups[2] = plus(groups[2], nt(r1_f[step(t)], hop_f[step(t), :]))
        groups[3] = plus(groups[3], nt(cot, hop_b[step(t), :]))
        groups[4] = plus(groups[4], nt(r1_b[step(t)], hop_b[step(t), :]))
        mix_bias = plus(mix_bias, nt(ones, cot))
    skip_grad = nt(cs_ref[...], hid[last, :])
    skip_bias = nt(ones, cs_ref[...])
    skips = skip_grad.shape[0]
    for g in range(5):
        put(early, g * chans, groups[g])
    put(early, 5 * chans, skip_grad)
    bias_top = 5 * chans + skips
    put(early, bias_top, mix_bias)
    for g in range(skips // 128):
        put(early, bias_top + 16 * (g + 1), skip_bias[:, lanes(g, 128)])

    def scatter(buffer, landing, base):
        return [
            send(buffer.at[peer], landing.at[k], red_sem, (base + k,), {"batch": peer})
            for k, peer in enumerate(mates)
        ]

    def across(buffer, landing, nodes, copies, base):
        total = buffer[row].astype(F32)
        for k, copy in enumerate(copies):
            copy.wait_recv()
            total += landing[k].astype(F32)
        nodes[me] = total.astype(BF16)
        return [
            send(nodes.at[me], nodes.at[me], red_sem, (base + k,), {"node": peer})
            for k, peer in enumerate(ahead)
        ]

    def arrived(copies, nodes, sem_base):
        for k, peer in enumerate(behind):
            pltpu.make_async_remote_copy(
                src_ref=nodes.at[peer], dst_ref=nodes.at[peer],
                send_sem=red_sem.at[0, sem_base + k], recv_sem=red_sem.at[1, sem_base + k],
                device_id={"node": peer}, device_id_type=MESH,
            ).wait_recv()

    def gather(nodes, result, base):
        total = nodes[0].astype(F32)
        for k in range(1, n_node):
            total += nodes[k].astype(F32)
        result[row] = total.astype(BF16)
        return [
            send(result.at[row], result.at[row], red_sem, (base + k,), {"batch": peer})
            for k, peer in enumerate(mates)
        ]

    def gathered(result, base):
        for k in range(n_batch - 1):
            peer = lax.rem(row + n_batch - k - 1, n_batch)
            pltpu.make_async_remote_copy(
                src_ref=result.at[peer], dst_ref=result.at[peer],
                send_sem=red_sem.at[0, base + k], recv_sem=red_sem.at[1, base + k],
                device_id={"batch": peer}, device_id_type=MESH,
            ).wait_recv()

    span = 2 * (n_batch - 1) + n_node - 1
    at1, at2 = n_batch - 1, n_batch - 1 + n_node - 1
    early_copies = scatter(early, early_rs, 0)

    near_one = base0[...] + nn(one_f[...], dense_f[...]) + nn(one_b[...], dense_b[...])
    near_u = mix0[...] + nt(u_f[...], dense_f[...]) + nt(u_b[...], dense_b[...])

    early_node_copies = across(early, early_rs, early_node, early_copies, at1)

    for copy in back_copies:
        copy.wait_recv()
    conv_grad = None
    conv_bias = None
    placed = []
    for j in range(blocks):
        total = near_one[:, lanes(j, width)]
        for k in range(n_node - 1):
            total += back_in[k].astype(F32) * pick_mask(src_rows[k], j)
        placed.append(total)
    grad_hidden = jnp.concatenate(placed, axis=1).astype(BF16).astype(F32)
    for t in range(steps):
        f, s, g = filt[step(t), :], gate[step(t), :], grad_hidden[step(t)]
        gs = g * s
        both = jnp.concatenate([gs * (1.0 - f * f), gs * f * (1.0 - s)], axis=0).astype(BF16)
        pre[t] = both
        conv_grad = plus(conv_grad, nt(both, taps[t]))
        conv_bias = plus(conv_bias, nt(ones, both))
    put(late, 0, conv_grad)
    put(late, 2 * chans, conv_bias)
    late_copies = scatter(late, late_rs, span)

    arrived(early_node_copies, early_node, at1)
    gather(early_node, early_all, at2)

    for t in range(steps + DILATION_GAP):
        total = None
        if t < steps:
            total = nn(conv_t[:chans], pre[t])
        if t >= DILATION_GAP:
            total = plus(total, nn(conv_t[chans:], pre[t - DILATION_GAP]))
            total += rc_ref[step(t - DILATION_GAP), :].astype(F32)
        gx_ref[step(t), :] = total.astype(BF16)

    late_node_copies = across(late, late_rs, late_node, late_copies, span + at1)

    for copy in two_copies:
        copy.wait_recv()
    mix_col = jnp.broadcast_to(
        jnp.concatenate([bm_ref[...]] * (128 // chans), axis=1), (128, 128)
    ).T
    mix_col = jnp.concatenate([mix_col[:chans]] * steps, axis=0)
    for i in range(blocks):
        total = near_u[:, lanes(i, width)] + mix_col
        for k in range(n_node - 1):
            total += two_in[k].astype(F32) * dst_masks[k][i]
        total += x_ref[DILATION_GAP * chans :, lanes(i, width)].astype(F32)
        res_ref[:, lanes(i, width)] = total.astype(BF16)

    arrived(late_node_copies, late_node, span + at1)
    gather(late_node, late_all, span + at2)

    gathered(early_all, at2)
    for g in range(5):
        gwm_ref[:, lanes(g, chans)] = take(early_all, g * chans, chans, chans) * scale
    gws_ref[...] = take(early_all, 5 * chans, skips, chans) * scale
    gbm_ref[...] = take(early_all, bias_top, 16, chans)[0:1] * scale
    for g in range(skips // 128):
        gbs_ref[:, lanes(g, 128)] = take(early_all, bias_top + 16 * (g + 1), 16, 128)[0:1] * scale
    gathered(late_all, span + at2)
    gwc_ref[...] = take(late_all, 0, 2 * chans, 2 * chans) * scale
    gbc_ref[...] = take(late_all, 2 * chans, 16, 2 * chans)[0:1] * scale

    for copy in started:
        copy.wait_send()


def shards(
    inputs, w_conv, b_conv, w_mix, b_mix, w_skip, b_skip, local_fwd, local_bwd,
    remote_fwd, remote_bwd, tile_src, tile_dst, residual_cotangent, cot_skip,
):
    n_node, n_batch = lax.axis_size("node"), lax.axis_size("batch")
    windows, input_steps, chans, local_nodes = inputs.shape
    steps = input_steps - DILATION_GAP
    width = remote_fwd.shape[1]
    skips = w_skip.shape[0]
    rows = steps * chans
    scale = 1.0 / math.sqrt(float(windows * n_batch * local_nodes * n_node * steps))
    peers = n_node - 1

    def chunk(total):
        return -(-total // (16 * n_batch)) * 16

    early = chunk(5 * chans + skips + 16 * (1 + skips // 128))
    late = chunk(2 * chans + 16)

    def field(kind):
        return pltpu.VMEM((rows, local_nodes), kind)

    def slots(*shape):
        return pltpu.VMEM((peers, *shape), BF16)

    scratch = (
        [pltpu.VMEM((local_nodes, local_nodes), BF16)] * 2
        + [pltpu.VMEM((peers * width, local_nodes), BF16)] * 2
        + [pltpu.VMEM((local_nodes, peers * width), BF16)] * 2
        + [pltpu.VMEM((peers, 8, 128), jnp.int32)] * 2
        + [pltpu.VMEM((2, peers, width, width), BF16)]
        + [slots(rows, width)] * 8
        + [field(F32), field(F32), field(BF16)]
        + [pltpu.VMEM((steps, 2 * chans, local_nodes), BF16)]
        + [field(F32)] * 8
        + [field(BF16)] * 6
    )
    for size in (early, late):
        scratch += [
            pltpu.VMEM((n_batch, size, 128), BF16),
            pltpu.VMEM((n_batch - 1, size, 128), BF16),
            pltpu.VMEM((n_node, size, 128), BF16),
            pltpu.VMEM((n_batch, size, 128), BF16),
        ]
    scratch += [
        pltpu.SemaphoreType.DMA((2, 2, peers)),
        pltpu.SemaphoreType.DMA((2, 5, peers)),
        pltpu.SemaphoreType.DMA((2, 2 * (2 * (n_batch - 1) + peers))),
    ]
    vmem = pl.BlockSpec(memory_space=pltpu.VMEM)
    smem = pl.BlockSpec(memory_space=pltpu.SMEM)
    results = pl.pallas_call(
        functools.partial(kernel, (n_node, n_batch, steps, chans, scale)),
        out_shape=[
            jax.ShapeDtypeStruct((rows, local_nodes), BF16),
            jax.ShapeDtypeStruct((skips, local_nodes), BF16),
            jax.ShapeDtypeStruct((input_steps * chans, local_nodes), BF16),
            jax.ShapeDtypeStruct((2 * chans, 2 * chans), F32),
            jax.ShapeDtypeStruct((1, 2 * chans), F32),
            jax.ShapeDtypeStruct((chans, 5 * chans), F32),
            jax.ShapeDtypeStruct((1, chans), F32),
            jax.ShapeDtypeStruct((skips, chans), F32),
            jax.ShapeDtypeStruct((1, skips), F32),
        ],
        in_specs=[vmem] * 11 + [smem] * 2 + [vmem] * 2,
        out_specs=[vmem] * 9,
        scratch_shapes=scratch,
        compiler_params=pltpu.CompilerParams(
            collective_id=0, has_side_effects=True, vmem_limit_bytes=56 * 1024 * 1024
        ),
        cost_estimate=pl.CostEstimate(
            flops=2_000_000_000, bytes_accessed=4_000_000, transcendentals=300_000
        ),
    )(
        inputs.reshape(input_steps * chans, local_nodes),
        w_conv, b_conv[None], w_mix, b_mix[None], w_skip, b_skip[None],
        local_fwd, local_bwd, remote_fwd, remote_bwd, tile_src, tile_dst,
        residual_cotangent.reshape(rows, local_nodes),
        cot_skip.reshape(skips, local_nodes),
    )
    res, skip, gx, gwc, gbc, gwm, gbm, gws, gbs = results
    return (
        res.reshape(windows, steps, chans, local_nodes),
        skip.reshape(windows, skips, local_nodes),
        gx.reshape(windows, input_steps, chans, local_nodes),
        gwc, gbc[0], gwm, gbm[0], gws, gbs[0],
    )


def solution(mesh):
    return jax.shard_map(
        shards,
        mesh=mesh,
        in_specs=(
            P("batch", None, None, "node"),
            P(), P(), P(), P(), P(), P(),
            P("node", None),
            P("node", None),
            P("node", None, None),
            P("node", None, None),
            P("node"),
            P("node"),
            P("batch", None, None, "node"),
            P("batch", None, "node"),
        ),
        out_specs=(
            P("batch", None, None, "node"),
            P("batch", None, "node"),
            P("batch", None, None, "node"),
            P(), P(), P(), P(), P(), P(),
        ),
        check_vma=False,
    )
```

time: 357 us -> 49.2 us (0.14)
  waiting for transfers between devices: 134 us -> 0 us
  local copies, waits for them, and re-layouts: 67.5 us -> 9.8 us
  matrix products: 46.4 us -> 0 us
  blocking collectives: 39.6 us -> 0 us
  Pallas kernels: 0 us -> 38.3 us
  starting transfers between devices: 37.6 us -> 0 us
  other arithmetic: 14.5 us -> 0 us
  between operations: 14.7 us -> 0.66 us
    psum x1 -> x0, waiting for transfers between devices: 124 us -> none  [shards(): lax.psum((grad_wconv, grad_bconv, grad_mix, grad_bmix, grad_skip, grad_bs...]
    dot_general x39 -> x0, matrix products: 46.4 us -> none  [the longest x7 10.2 us: place_blocks(): jnp.einsum('qi,qmc->mic', chooser, pieces, preferred_element_type=jnp.flo...]
    psum x1 -> x0, blocking collectives: 39.6 us -> none  [shards(): lax.psum((grad_wconv, grad_bconv, grad_mix, grad_bmix, grad_skip, grad_bs...]
    pallas_call x0 -> x1, Pallas kernels: none -> 38.3 us  [shards(): pl.pallas_call(functools.partial(kernel, (n_node, n_batch, steps, chans,...]
    all_to_all x9 -> x0, starting transfers between devices: 37.6 us -> none  [the longest x2 8.42 us: push_hop(): lax.all_to_all(part_bwd, 'node', split_axis=0, concat_axis=0, tiled=True)]
    convert_element_type x14 -> x0, local copies, waits for them, and re-layouts: 11.1 us -> none  [the longest x4 3.98 us: pick_blocks(): jnp.einsum('qi,mic->qmc', chooser, shaped, preferred_element_type=jnp.flo...]
    slice x11 -> x0, local copies, waits for them, and re-layouts: 10.2 us -> none  [the longest x2 3.05 us: band_transpose(): from_after = jnp.concatenate([spread[:, 1:, 0], zeros_blk], axis=1)]
    all_to_all x9 -> x0, waiting for transfers between devices: 9.89 us -> none  [the longest x2 4.34 us: fetch_rows(): lax.all_to_all(pick_blocks(grad_bwd, recv_dst), 'node', split_axis=0, con...]
  transfers between devices with their start and end apart: 10 -> 0, of which waited for: 5 -> 0; matrix products, arithmetic and copies ran while one was open for 32% -> 0% of each run, Pallas kernels for 0% -> 0%
where the time goes in v1:
time: 49.2 us; the launch traced here: 48.8 us
  Pallas kernels  38.3 us (78%)
  local copies, waits for them, and re-layouts  9.8 us (20%)
  between operations  0.66 us (1%)
    pallas_call x1, Pallas kernels, shards(): pl.pallas_call(functools.partial(kernel, (n_node, n_batch, steps, chans,...  38.3 us
    unnamed x24, local copies, waits for them, and re-layouts  9.8 us

profile of v1, /device:TPU:0, one launch (start us, length us, event | category | flops | bytes accessed | tf_op | source)
XLA Modules:
  0.0 48.8 jit_solution(10911293493359190323)
XLA Ops:
  0.6 1.5 %copy.24.ws_ref = bf16[256,64]{1,0:T(8,128)(2,1)} copy(bf16[256,64]{0,1:T(8,128)(2,1)} %param.20) | data formatting | bytes 65536 | tf_op args[5]
  2.1 38.3 %shard_map.214 = (bf16[256,512]{1,0:T(8,128)(2,1)}, bf16[256,512]{1,0:T(8,128)(2,1)}, bf16[384,512]{1,0:T(8,128)(2,1)}, f32[128,128]{1,0:T(8,128)}, f32[1,128]{1...) custom-call(bf16[384,512]{1,0:T(8,128)(2,1)} %bitcast.16, ...), custom_call_target="tpu_custom_call" | custom-call | flops 2000000000 | bytes 4000000 | tf_op jit(solution)/shard_map/pallas_call | solution.py:430
  40.5 1.6 %copy.25 = f32[256,64]{0,1:T(8,128)} copy(f32[256,64]{1,0:T(8,128)} %get-tuple-element.34) | data formatting | bytes 131072
  42.1 0.0 copy-start.1
  42.1 1.7 %copy.34 = bf16[1,4,64,512]{3,2,1,0:T(8,128)(2,1)} copy(bf16[1,4,64,512]{3,2,1,0:T(8,128)(2,1)} %bitcast.14) | data formatting | bytes 524288
  43.8 0.0 copy-done.1
  43.8 0.0 copy-start
  43.8 0.7 %copy.35 = bf16[1,256,512]{2,1,0:T(8,128)(2,1)} copy(bf16[1,256,512]{2,1,0:T(8,128)(2,1)S(1)} %bitcast.13) | data formatting | bytes 524288
  44.5 0.4 copy-done
  44.9 0.0 copy-start.3
  44.9 0.7 %copy.36 = bf16[1,6,64,512]{3,2,1,0:T(8,128)(2,1)} copy(bf16[1,6,64,512]{3,2,1,0:T(8,128)(2,1)S(1)} %bitcast.12) | data formatting | bytes 786432
  45.6 0.1 copy-done.3
  45.7 0.0 copy-start.6
  45.7 0.0 copy-start.2
  45.7 0.6 %copy.37 = f32[128,128]{1,0:T(8,128)} copy(f32[128,128]{1,0:T(8,128)S(1)} %copy-done.3) | data formatting | bytes 131072
  46.4 0.0 copy-done.6
  46.4 0.5 %copy.38 = f32[128]{0:T(128)} copy(f32[128]{0:T(128)S(1)} %bitcast.23) | data formatting | bytes 1024
  46.9 0.0 copy-done.2
  46.9 0.0 copy-start.5
  46.9 0.6 %copy.39 = f32[64,320]{1,0:T(8,128)} copy(f32[64,320]{1,0:T(8,128)S(1)} %copy-done.2) | data formatting | bytes 163840
  47.5 0.0 copy-done.5
  47.5 0.0 copy-start.4
  47.5 0.5 %copy.40 = f32[64]{0:T(128)} copy(f32[64]{0:T(128)S(1)} %bitcast.22) | data formatting | bytes 512
  48.1 0.2 copy-done.4
  48.2 0.6 %copy.41 = f32[256]{0:T(256)} copy(f32[256]{0:T(256)S(1)} %bitcast.15) | data formatting | bytes 2048
Async XLA Ops:
  42.1 1.7 %copy-start.1 = (bf16[256,512]{1,0:T(8,128)(2,1)S(1)}, bf16[256,512]{1,0:T(8,128)(2,1)}, u32[]{:S(2)}) copy-start(bf16[256,512]{1,0:T(8,128)(2,1)} %get-tuple-element.19) | copy-start | bytes 786436
  43.8 1.1 %copy-start = (bf16[384,512]{1,0:T(8,128)(2,1)S(1)}, bf16[384,512]{1,0:T(8,128)(2,1)}, u32[]{:S(2)}) copy-start(bf16[384,512]{1,0:T(8,128)(2,1)} %get-tuple-element.20) | copy-start | bytes 1179652
  44.9 0.9 %copy-start.3 = (f32[128,128]{1,0:T(8,128)S(1)}, f32[128,128]{1,0:T(8,128)}, u32[]{:S(2)}) copy-start(f32[128,128]{1,0:T(8,128)} %get-tuple-element.48) | copy-start | bytes 196612
  45.7 0.6 %copy-start.6 = (f32[1,128]{1,0:T(1,128)S(1)}, f32[1,128]{1,0:T(1,128)}, u32[]{:S(2)}) copy-start(f32[1,128]{1,0:T(1,128)} %get-tuple-element.22) | copy-start | bytes 1540
  45.7 1.1 %copy-start.2 = (f32[64,320]{1,0:T(8,128)S(1)}, f32[64,320]{1,0:T(8,128)}, u32[]{:S(2)}) copy-start(f32[64,320]{1,0:T(8,128)} %get-tuple-element.50) | copy-start | bytes 245764
  46.9 0.6 %copy-start.5 = (f32[1,64]{1,0:T(1,128)S(1)}, f32[1,64]{1,0:T(1,128)}, u32[]{:S(2)}) copy-start(f32[1,64]{1,0:T(1,128)} %get-tuple-element.24) | copy-start | bytes 772
  47.5 0.7 %copy-start.4 = (f32[1,256]{1,0:T(1,128)S(1)}, f32[1,256]{1,0:T(1,128)}, u32[]{:S(2)}) copy-start(f32[1,256]{1,0:T(1,128)} %get-tuple-element.26) | copy-start | bytes 3076

commit v2 on v1

--- a/solution.py
+++ b/solution.py
@@ -40,7 +40,7 @@
     sizes,
     x_ref, wc_ref, bc_ref, wm_ref, bm_ref, ws_ref, bs_ref, lf_ref, lb_ref, rf_ref, rb_ref,
     src_ref, dst_ref, rc_ref, cs_ref,
-    res_ref, skip_ref, gx_ref, gwc_ref, gbc_ref, gwm_ref, gbm_ref, gws_ref, gbs_ref,
+    res_ref, skip_ref, gx_ref, early_ref, late_ref,
     dense_f, dense_b, hold_f, hold_b, far_f, far_b,
     dst_out, dst_in, tile_in,
     h_out, h_in, rc_out, rc_in, back_out, back_in, two_out, two_in,
@@ -145,7 +145,8 @@
 
     mix_t = nt(identity(5 * chans), wm_ref[...]).astype(BF16)
     conv_t = nt(identity(2 * chans), wc_ref[...]).astype(BF16)
-    skip_t = nt(identity(chans), ws_ref[...]).astype(BF16)
+    skips = ws_ref.shape[1]
+    skip_w = nt(identity(skips), ws_ref[...]).astype(BF16)
     mix_w = [wm_ref[:, lanes(g, chans)] for g in range(5)]
 
     for t in range(steps):
@@ -158,13 +159,13 @@
         mix1[step(t), :] = nn(mix_w[1], h_t)
         mix3[step(t), :] = nn(mix_w[3], h_t)
     last = step(steps - 1)
-    base0[last, :] += nn(skip_t, cs_ref[...])
+    base0[last, :] += nn(ws_ref[...], cs_ref[...])
     near_f[...] = nn(rc_ref[...], dense_f[...])
     near_b[...] = nn(rc_ref[...], dense_b[...])
     hop_f32 = nt(hid[...], dense_f[...])
     hop_b32 = nt(hid[...], dense_b[...])
 
-    skip = nn(ws_ref[...], hid[last, :])
+    skip = nn(skip_w, hid[last, :])
     half = 128
     for g in range(skip.shape[0] // half):
         part = jnp.broadcast_to(bs_ref[:, lanes(g, half)], (half, half)).T
@@ -220,17 +221,6 @@
             buffer[c, o : o + n, 0 : value.shape[1]] = value[at - top : at - top + n]
             at += n
 
-    def take(buffer, top, count, cols):
-        rows = buffer.shape[1]
-        parts = []
-        at = top
-        while at < top + count:
-            c, o = at // rows, at % rows
-            n = min(rows - o, top + count - at)
-            parts.append(buffer[c, o : o + n, 0:cols].astype(F32))
-            at += n
-        return parts[0] if len(parts) == 1 else jnp.concatenate(parts, axis=0)
-
     groups = [None] * 5
     mix_bias = None
 
@@ -245,16 +235,18 @@
         groups[3] = plus(groups[3], nt(cot, hop_b[step(t), :]))
         groups[4] = plus(groups[4], nt(r1_b[step(t)], hop_b[step(t), :]))
         mix_bias = plus(mix_bias, nt(ones, cot))
-    skip_grad = nt(cs_ref[...], hid[last, :])
+    skip_grad = nt(hid[last, :], cs_ref[...])
     skip_bias = nt(ones, cs_ref[...])
-    skips = skip_grad.shape[0]
-    for g in range(5):
-        put(early, g * chans, groups[g])
-    put(early, 5 * chans, skip_grad)
-    bias_top = 5 * chans + skips
+    put(early, 0, jnp.concatenate([groups[0], groups[1]], axis=1))
+    put(early, chans, jnp.concatenate([groups[2], groups[3]], axis=1))
+    put(early, 2 * chans, groups[4])
+    bias_top = 3 * chans
     put(early, bias_top, mix_bias)
     for g in range(skips // 128):
         put(early, bias_top + 16 * (g + 1), skip_bias[:, lanes(g, 128)])
+    skip_top = bias_top + 16 * (1 + skips // 128)
+    for g in range(skips // 128):
+        put(early, skip_top + g * chans, skip_grad[:, lanes(g, 128)])
 
     def scatter(buffer, landing, base):
         return [
@@ -362,18 +354,50 @@
     gather(late_node, late_all, span + at2)
 
     gathered(early_all, at2)
-    for g in range(5):
-        gwm_ref[:, lanes(g, chans)] = take(early_all, g * chans, chans, chans) * scale
-    gws_ref[...] = take(early_all, 5 * chans, skips, chans) * scale
-    gbm_ref[...] = take(early_all, bias_top, 16, chans)[0:1] * scale
-    for g in range(skips // 128):
-        gbs_ref[:, lanes(g, 128)] = take(early_all, bias_top + 16 * (g + 1), 16, 128)[0:1] * scale
+    early_ref[...] = early_all[...]
     gathered(late_all, span + at2)
-    gwc_ref[...] = take(late_all, 0, 2 * chans, 2 * chans) * scale
-    gbc_ref[...] = take(late_all, 2 * chans, 16, 2 * chans)[0:1] * scale
+    late_ref[...] = late_all[...]
 
     for copy in started:
         copy.wait_send()
+
+
+def finish(
+    sizes, res_in, skip_in, gx_in, early, late,
+    res_ref, skip_ref, gx_ref, gwc_ref, gbc_ref, gwm_ref, gbm_ref, gws_ref, gbs_ref, sems,
+):
+    chans, skips, scale = sizes
+    copies = [
+        pltpu.make_async_copy(a, b, sems.at[k])
+        for k, (a, b) in enumerate(((res_in, res_ref), (skip_in, skip_ref), (gx_in, gx_ref)))
+    ]
+    for copy in copies:
+        copy.start()
+
+    def take(buffer, top, count):
+        rows = buffer.shape[1]
+        parts = []
+        at = top
+        while at < top + count:
+            c, o = at // rows, at % rows
+            n = min(rows - o, top + count - at)
+            parts.append(buffer[c, o : o + n, :].astype(F32))
+            at += n
+        return (parts[0] if len(parts) == 1 else jnp.concatenate(parts, axis=0)) * scale
+
+    gwm_ref[:, : 2 * chans] = take(early, 0, chans)
+    gwm_ref[:, 2 * chans : 4 * chans] = take(early, chans, chans)
+    gwm_ref[:, 4 * chans :] = take(early, 2 * chans, chans)[:, :chans]
+    bias_top = 3 * chans
+    gbm_ref[...] = take(early, bias_top, 16)[0:1, :chans]
+    skip_top = bias_top + 16 * (1 + skips // 128)
+    for g in range(skips // 128):
+        gbs_ref[:, lanes(g, 128)] = take(early, bias_top + 16 * (g + 1), 16)[0:1]
+        gws_ref[:, lanes(g, 128)] = take(early, skip_top + g * chans, chans)
+    gwc_ref[...] = take(late, 0, 2 * chans)
+    gbc_ref[...] = take(late, 2 * chans, 16)[0:1]
+    for copy in copies:
+        copy.wait()
 
 
 def shards(
@@ -392,7 +416,7 @@
     def chunk(total):
         return -(-total // (16 * n_batch)) * 16
 
-    early = chunk(5 * chans + skips + 16 * (1 + skips // 128))
+    early = chunk(3 * chans + 16 * (1 + skips // 128) + skips // 128 * chans)
     late = chunk(2 * chans + 16)
 
     def field(kind):
@@ -433,15 +457,11 @@
             jax.ShapeDtypeStruct((rows, local_nodes), BF16),
             jax.ShapeDtypeStruct((skips, local_nodes), BF16),
             jax.ShapeDtypeStruct((input_steps * chans, local_nodes), BF16),
-            jax.ShapeDtypeStruct((2 * chans, 2 * chans), F32),
-            jax.ShapeDtypeStruct((1, 2 * chans), F32),
-            jax.ShapeDtypeStruct((chans, 5 * chans), F32),
-            jax.ShapeDtypeStruct((1, chans), F32),
-            jax.ShapeDtypeStruct((skips, chans), F32),
-            jax.ShapeDtypeStruct((1, skips), F32),
+            jax.ShapeDtypeStruct((n_batch, early, 128), BF16),
+            jax.ShapeDtypeStruct((n_batch, late, 128), BF16),
         ],
         in_specs=[vmem] * 11 + [smem] * 2 + [vmem] * 2,
-        out_specs=[vmem] * 9,
+        out_specs=[vmem] * 5,
         scratch_shapes=scratch,
         compiler_params=pltpu.CompilerParams(
             collective_id=0, has_side_effects=True, vmem_limit_bytes=56 * 1024 * 1024
@@ -451,17 +471,33 @@
         ),
     )(
         inputs.reshape(input_steps * chans, local_nodes),
-        w_conv, b_conv[None], w_mix, b_mix[None], w_skip, b_skip[None],
+        w_conv, b_conv[None], w_mix, b_mix[None], w_skip.T, b_skip[None],
         local_fwd, local_bwd, remote_fwd, remote_bwd, tile_src, tile_dst,
         residual_cotangent.reshape(rows, local_nodes),
         cot_skip.reshape(skips, local_nodes),
     )
-    res, skip, gx, gwc, gbc, gwm, gbm, gws, gbs = results
+    anywhere = pl.BlockSpec(memory_space=pl.ANY)
+    res, skip, gx, gwc, gbc, gwm, gbm, gws, gbs = pl.pallas_call(
+        functools.partial(finish, (chans, skips, scale)),
+        out_shape=[
+            *[jax.ShapeDtypeStruct(a.shape, a.dtype) for a in results[:3]],
+            jax.ShapeDtypeStruct((2 * chans, 2 * chans), F32),
+            jax.ShapeDtypeStruct((1, 2 * chans), F32),
+            jax.ShapeDtypeStruct((chans, 5 * chans), F32),
+            jax.ShapeDtypeStruct((1, chans), F32),
+            jax.ShapeDtypeStruct((chans, skips), F32),
+            jax.ShapeDtypeStruct((1, skips), F32),
+        ],
+        in_specs=[anywhere] * 3 + [vmem] * 2,
+        out_specs=[anywhere] * 3 + [vmem] * 6,
+        scratch_shapes=[pltpu.SemaphoreType.DMA((3,))],
+        compiler_params=pltpu.CompilerParams(vmem_limit_bytes=56 * 1024 * 1024),
+    )(*results)
     return (
         res.reshape(windows, steps, chans, local_nodes),
         skip.reshape(windows, skips, local_nodes),
         gx.reshape(windows, input_steps, chans, local_nodes),
-        gwc, gbc[0], gwm, gbm[0], gws, gbs[0],
+        gwc, gbc[0], gwm, gbm[0], gws.T, gbs[0],
     )
 
 

time: 49.2 us -> 69.6 us (1.41)
  Pallas kernels: 38.3 us -> 68.8 us
  local copies, waits for them, and re-layouts: 9.8 us -> 0 us
    pallas_call x0 -> x1, Pallas kernels: none -> 30.5 us  [shards(): pl.pallas_call(functools.partial(finish, (chans, skips, scale)), out_shap...]
    unnamed x24 -> x0, local copies, waits for them, and re-layouts: 9.8 us -> none
where the time goes in v2:
time: 69.6 us; the launch traced here: 69.4 us
  Pallas kernels  68.8 us (99%)
    pallas_call x1, Pallas kernels, shards(): pl.pallas_call(functools.partial(kernel, (n_node, n_batch, steps, chans,...  38.3 us
    pallas_call x1, Pallas kernels, shards(): pl.pallas_call(functools.partial(finish, (chans, skips, scale)), out_shap...  30.5 us

profile of v2, /device:TPU:0, one launch (start us, length us, event | category | flops | bytes accessed | tf_op | source)
XLA Modules:
  0.0 69.4 jit_solution(12397779649588503257)
XLA Ops:
  0.6 38.3 %shard_map.214 = (bf16[256,512]{1,0:T(8,128)(2,1)}, bf16[256,512]{1,0:T(8,128)(2,1)}, bf16[384,512]{1,0:T(8,128)(2,1)}, bf16[8,48,128]{2,1,0:T(8,128)(2,1)}, bf16[8,32,128]{2,1,0:T(8,128)(2,1)}) custom-call(bf16[384,512]{1,0:T(8,128)(2,1)} %bitcast.14, bf16[128,128]{1,0:T(8,128)(2,1)} %wc_ref.1, f32[1,128]{1,0:T(1,128)} %bitcast.24, bf16[64,320]{1,0:T(8,128)(2,1)} %wm_ref.1, ...), custom_call_target="tpu_custom_call" | custom-call | flops 2000000000 | bytes 4000000 | tf_op jit(solution)/shard_map/pallas_call | solution.py:454
  38.9 30.5 %shard_map.215 = (bf16[256,512]{1,0:T(8,128)(2,1)}, bf16[256,512]{1,0:T(8,128)(2,1)}, bf16[384,512]{1,0:T(8,128)(2,1)}, f32[128,128]{1,0:T(8,128)}, f32[1,128]{1...) custom-call(bf16[256,512]{1,0:T(8,128)(2,1)} %get-tuple-element.23.res_in, ...), custom_call_target="tpu_custom_call" | custom-call | tf_op jit(solution)/shard_map/pallas_call | solution.py:480

commit v3 on v2

--- a/solution.py
+++ b/solution.py
@@ -55,8 +55,7 @@
     me = lax.axis_index("node")
     row = lax.axis_index("batch")
     offsets = range(1, n_node)
-    ahead = [lax.rem(me + r, n_node) for r in offsets]
-    behind = [lax.rem(me + n_node - r, n_node) for r in offsets]
+    ahead = behind = [me ^ r for r in offsets]
     mates = [lax.rem(row + r, n_batch) for r in range(1, n_batch)]
 
     barrier = pltpu.get_barrier_semaphore()
@@ -94,29 +93,6 @@
         )
     src_rows = [jnp.full((1, width), src_ref[peer], jnp.int32) for peer in ahead]
 
-    hid_pick = [[pick_mask(src_rows[k], j).astype(BF16) for j in range(blocks)] for k in range(n_node - 1)]
-    bias = jnp.broadcast_to(bc_ref[...], (2 * chans, 2 * chans)).T
-    bias = jnp.concatenate([bias] * (blocks * width // (2 * chans)), axis=1)
-    taps = [
-        jnp.concatenate([x_ref[step(t), :], x_ref[step(t + DILATION_GAP), :]], axis=0)
-        for t in range(steps)
-    ]
-    for t in range(steps):
-        act = nn(wc_ref[...], taps[t]) + bias
-        f = jnp.tanh(act[:chans])
-        s = jax.nn.sigmoid(act[chans:])
-        filt[step(t), :] = f
-        gate[step(t), :] = s
-        hid[step(t), :] = (f * s).astype(BF16)
-
-    h_copies = []
-    for k, peer in enumerate(ahead):
-        picked = hid[:, lanes(0, width)] * hid_pick[k][0]
-        for j in range(1, blocks):
-            picked += hid[:, lanes(j, width)] * hid_pick[k][j]
-        h_out[k] = picked
-        h_copies.append(send(h_out.at[k], h_in.at[k], node_sem, (1, k), {"node": peer}))
-
     rc_copies = []
     dst_masks = []
     for k, peer in enumerate(behind):
@@ -128,6 +104,29 @@
             picked += rc_ref[:, lanes(i, width)] * dst_masks[k][i].astype(BF16)
         rc_out[k] = picked
         rc_copies.append(send(rc_out.at[k], rc_in.at[k], node_sem, (2, k), {"node": peer}))
+
+    hid_pick = [[pick_mask(src_rows[k], j).astype(BF16) for j in range(blocks)] for k in range(n_node - 1)]
+    bias = jnp.broadcast_to(bc_ref[...], (2 * chans, 2 * chans)).T
+    bias = jnp.concatenate([bias] * (blocks * width // (2 * chans)), axis=1)
+    taps = [
+        jnp.concatenate([x_ref[step(t), :], x_ref[step(t + DILATION_GAP), :]], axis=0)
+        for t in range(steps)
+    ]
+    for t in range(steps):
+        act = nn(wc_ref[...], taps[t]) + bias
+        f = jnp.tanh(act[:chans])
+        s = jax.nn.sigmoid(act[chans:])
+        filt[step(t), :] = f
+        gate[step(t), :] = s
+        hid[step(t), :] = (f * s).astype(BF16)
+
+    h_copies = []
+    for k, peer in enumerate(ahead):
+        picked = hid[:, lanes(0, width)] * hid_pick[k][0]
+        for j in range(1, blocks):
+            picked += hid[:, lanes(j, width)] * hid_pick[k][j]
+        h_out[k] = picked
+        h_copies.append(send(h_out.at[k], h_in.at[k], node_sem, (1, k), {"node": peer}))
 
     for dense, local in ((dense_f, lf_ref), (dense_b, lb_ref)):
         for i in range(blocks):
@@ -151,19 +150,59 @@
 
     for t in range(steps):
         cot = rc_ref[step(t), :]
-        base0[step(t), :] = nn(mix_t[lanes(0, chans)], cot)
         base1[step(t), :] = nn(mix_t[lanes(1, chans)], cot)
         base3[step(t), :] = nn(mix_t[lanes(3, chans)], cot)
+    near_f[...] = nn(rc_ref[...], dense_f[...])
+    near_b[...] = nn(rc_ref[...], dense_b[...])
+
+    for k in range(n_node - 1):
+        tile_copies[k][0].wait_recv()
+        tile_copies[k][1].wait_recv()
+        for i in range(blocks):
+            mask = dst_masks[k][i].astype(BF16)
+            far_f[lanes(i, width), lanes(k, width)] = tile_in[0, k] * mask
+            far_b[lanes(i, width), lanes(k, width)] = tile_in[1, k] * mask
+
+    for copy in rc_copies:
+        copy.wait_recv()
+    far_rc = jnp.concatenate([rc_in[k] for k in range(n_node - 1)], axis=1)
+    r1_f = (near_f[...] + nn(far_rc, hold_f[...])).astype(BF16)
+    r1_b = (near_b[...] + nn(far_rc, hold_b[...])).astype(BF16)
+    for t in range(steps):
+        one_f[step(t), :] = (base1[step(t), :] + nn(mix_t[lanes(2, chans)], r1_f[step(t)])).astype(BF16)
+        one_b[step(t), :] = (base3[step(t), :] + nn(mix_t[lanes(4, chans)], r1_b[step(t)])).astype(BF16)
+    terms = nn(one_f[...], far_f[...]) + nn(one_b[...], far_b[...])
+    back_copies = []
+    for k, peer in enumerate(behind):
+        back_out[k] = terms[:, lanes(k, width)].astype(BF16)
+        back_copies.append(send(back_out.at[k], back_in.at[k], node_sem, (4, k), {"node": peer}))
+
+    for t in range(steps):
         h_t = hid[step(t), :]
-        mix0[step(t), :] = nn(mix_w[0], h_t)
         mix1[step(t), :] = nn(mix_w[1], h_t)
         mix3[step(t), :] = nn(mix_w[3], h_t)
+    hop_f32 = nt(hid[...], dense_f[...])
+    hop_b32 = nt(hid[...], dense_b[...])
+
+    for copy in h_copies:
+        copy.wait_recv()
+    far_h = jnp.concatenate([h_in[k] for k in range(n_node - 1)], axis=1)
+    hop_f[...] = (hop_f32 + nt(far_h, far_f[...])).astype(BF16)
+    hop_b[...] = (hop_b32 + nt(far_h, far_b[...])).astype(BF16)
+    for t in range(steps):
+        u_f[step(t), :] = (mix1[step(t), :] + nn(mix_w[2], hop_f[step(t), :])).astype(BF16)
+        u_b[step(t), :] = (mix3[step(t), :] + nn(mix_w[4], hop_b[step(t), :])).astype(BF16)
+    terms = nt(u_f[...], hold_f[...]) + nt(u_b[...], hold_b[...])
+    two_copies = []
+    for k, peer in enumerate(ahead):
+        two_out[k] = terms[:, lanes(k, width)].astype(BF16)
+        two_copies.append(send(two_out.at[k], two_in.at[k], node_sem, (3, k), {"node": peer}))
+
+    for t in range(steps):
+        base0[step(t), :] = nn(mix_t[lanes(0, chans)], rc_ref[step(t), :])
+        mix0[step(t), :] = nn(mix_w[0], hid[step(t), :])
     last = step(steps - 1)
     base0[last, :] += nn(ws_ref[...], cs_ref[...])
-    near_f[...] = nn(rc_ref[...], dense_f[...])
-    near_b[...] = nn(rc_ref[...], dense_b[...])
-    hop_f32 = nt(hid[...], dense_f[...])
-    hop_b32 = nt(hid[...], dense_b[...])
 
     skip = nn(skip_w, hid[last, :])
     half = 128
@@ -174,42 +213,6 @@
     ones = jnp.ones((16, blocks * width), BF16)
     early[...] = jnp.zeros_like(early)
     late[...] = jnp.zeros_like(late)
-
-    for k in range(n_node - 1):
-        tile_copies[k][0].wait_recv()
-        tile_copies[k][1].wait_recv()
-        for i in range(blocks):
-            mask = dst_masks[k][i].astype(BF16)
-            far_f[lanes(i, width), lanes(k, width)] = tile_in[0, k] * mask
-            far_b[lanes(i, width), lanes(k, width)] = tile_in[1, k] * mask
-
-    for copy in h_copies:
-        copy.wait_recv()
-    far_h = jnp.concatenate([h_in[k] for k in range(n_node - 1)], axis=1)
-    hop_f[...] = (hop_f32 + nt(far_h, far_f[...])).astype(BF16)
-    hop_b[...] = (hop_b32 + nt(far_h, far_b[...])).astype(BF16)
-    for t in range(steps):
-        u_f[step(t), :] = (mix1[step(t), :] + nn(mix_w[2], hop_f[step(t), :])).astype(BF16)
-        u_b[step(t), :] = (mix3[step(t), :] + nn(mix_w[4], hop_b[step(t), :])).astype(BF16)
-    terms = nt(u_f[...], hold_f[...]) + nt(u_b[...], hold_b[...])
-    two_copies = []
-    for k, peer in enumerate(ahead):
-        two_out[k] = terms[:, lanes(k, width)].astype(BF16)
-        two_copies.append(send(two_out.at[k], two_in.at[k], node_sem, (3, k), {"node": peer}))
-
-    for copy in rc_copies:
-        copy.wait_recv()
-    far_rc = jnp.concatenate([rc_in[k] for k in range(n_node - 1)], axis=1)
-    r1_f = (near_f[...] + nn(far_rc, hold_f[...])).astype(BF16)
-    r1_b = (near_b[...] + nn(far_rc, hold_b[...])).astype(BF16)
-    for t in range(steps):
-        one_f[step(t), :] = (base1[step(t), :] + nn(mix_t[lanes(2, chans)], r1_f[step(t)])).astype(BF16)
-        one_b[step(t), :] = (base3[step(t), :] + nn(mix_t[lanes(4, chans)], r1_b[step(t)])).astype(BF16)
-    terms = nn(one_f[...], far_f[...]) + nn(one_b[...], far_b[...])
-    back_copies = []
-    for k, peer in enumerate(behind):
-        back_out[k] = terms[:, lanes(k, width)].astype(BF16)
-        back_copies.append(send(back_out.at[k], back_in.at[k], node_sem, (4, k), {"node": peer}))
 
     def put(buffer, top, value):
         rows = buffer.shape[1]
@@ -299,8 +302,6 @@
     near_one = base0[...] + nn(one_f[...], dense_f[...]) + nn(one_b[...], dense_b[...])
     near_u = mix0[...] + nt(u_f[...], dense_f[...]) + nt(u_b[...], dense_b[...])
 
-    early_node_copies = across(early, early_rs, early_node, early_copies, at1)
-
     for copy in back_copies:
         copy.wait_recv()
     conv_grad = None
@@ -322,9 +323,7 @@
     put(late, 0, conv_grad)
     put(late, 2 * chans, conv_bias)
     late_copies = scatter(late, late_rs, span)
-
-    arrived(early_node_copies, early_node, at1)
-    gather(early_node, early_all, at2)
+    early_node_copies = across(early, early_rs, early_node, early_copies, at1)
 
     for t in range(steps + DILATION_GAP):
         total = None
@@ -336,6 +335,9 @@
         gx_ref[step(t), :] = total.astype(BF16)
 
     late_node_copies = across(late, late_rs, late_node, late_copies, span + at1)
+
+    arrived(early_node_copies, early_node, at1)
+    gather(early_node, early_all, at2)
 
     for copy in two_copies:
         copy.wait_recv()
@@ -364,15 +366,12 @@
 
 def finish(
     sizes, res_in, skip_in, gx_in, early, late,
-    res_ref, skip_ref, gx_ref, gwc_ref, gbc_ref, gwm_ref, gbm_ref, gws_ref, gbs_ref, sems,
+    res_ref, skip_ref, gx_ref, gwc_ref, gbc_ref, gwm_ref, gbm_ref, gws_ref, gbs_ref,
 ):
     chans, skips, scale = sizes
-    copies = [
-        pltpu.make_async_copy(a, b, sems.at[k])
-        for k, (a, b) in enumerate(((res_in, res_ref), (skip_in, skip_ref), (gx_in, gx_ref)))
-    ]
-    for copy in copies:
-        copy.start()
+    res_ref[...] = res_in[...]
+    skip_ref[...] = skip_in[...]
+    gx_ref[...] = gx_in[...]
 
     def take(buffer, top, count):
         rows = buffer.shape[1]
@@ -396,8 +395,6 @@
         gws_ref[:, lanes(g, 128)] = take(early, skip_top + g * chans, chans)
     gwc_ref[...] = take(late, 0, 2 * chans)
     gbc_ref[...] = take(late, 2 * chans, 16)[0:1]
-    for copy in copies:
-        copy.wait()
 
 
 def shards(
@@ -476,7 +473,6 @@
         residual_cotangent.reshape(rows, local_nodes),
         cot_skip.reshape(skips, local_nodes),
     )
-    anywhere = pl.BlockSpec(memory_space=pl.ANY)
     res, skip, gx, gwc, gbc, gwm, gbm, gws, gbs = pl.pallas_call(
         functools.partial(finish, (chans, skips, scale)),
         out_shape=[
@@ -488,9 +484,8 @@
             jax.ShapeDtypeStruct((chans, skips), F32),
             jax.ShapeDtypeStruct((1, skips), F32),
         ],
-        in_specs=[anywhere] * 3 + [vmem] * 2,
-        out_specs=[anywhere] * 3 + [vmem] * 6,
-        scratch_shapes=[pltpu.SemaphoreType.DMA((3,))],
+        in_specs=[vmem] * 5,
+        out_specs=[vmem] * 9,
         compiler_params=pltpu.CompilerParams(vmem_limit_bytes=56 * 1024 * 1024),
     )(*results)
     return (

time: 69.6 us -> 38.1 us (0.55)
  Pallas kernels: 68.8 us -> 37.3 us
    pallas_call x1, Pallas kernels: 30.5 us -> 2.23 us  [shards(): pl.pallas_call(functools.partial(finish, (chans, skips, scale)), out_shap...]
    pallas_call x1, Pallas kernels: 38.3 us -> 35.1 us  [shards(): pl.pallas_call(functools.partial(kernel, (n_node, n_batch, steps, chans,...]
where the time goes in v3:
time: 38.1 us; the launch traced here: 38 us
  Pallas kernels  37.3 us (98%)
  between operations  0.66 us (2%)
    pallas_call x1, Pallas kernels, shards(): pl.pallas_call(functools.partial(kernel, (n_node, n_batch, steps, chans,...  35.1 us
    pallas_call x1, Pallas kernels, shards(): pl.pallas_call(functools.partial(finish, (chans, skips, scale)), out_shap...  2.23 us

profile of v3, /device:TPU:0, one launch (start us, length us, event | category | flops | bytes accessed | tf_op | source)
XLA Modules:
  0.0 38.0 jit_solution(10217647652060953679)
XLA Ops:
  0.6 35.1 %shard_map.214 = (bf16[256,512]{1,0:T(8,128)(2,1)}, bf16[256,512]{1,0:T(8,128)(2,1)}, bf16[384,512]{1,0:T(8,128)(2,1)}, bf16[8,48,128]{2,1,0:T(8,128)(2,1)}, bf16[8,32,128]{2,1,0:T(8,128)(2,1)}) custom-call(bf16[384,512]{1,0:T(8,128)(2,1)} %bitcast.14, bf16[128,128]{1,0:T(8,128)(2,1)} %wc_ref.1, f32[1,128]{1,0:T(1,128)} %bitcast.24, bf16[64,320]{1,0:T(8,128)(2,1)} %wm_ref.1, ...), custom_call_target="tpu_custom_call" | custom-call | flops 2000000000 | bytes 4000000 | tf_op jit(solution)/shard_map/pallas_call | solution.py:451
  35.7 2.2 %shard_map.215 = (bf16[256,512]{1,0:T(8,128)(2,1)}, bf16[256,512]{1,0:T(8,128)(2,1)}, bf16[384,512]{1,0:T(8,128)(2,1)}, f32[128,128]{1,0:T(8,128)}, f32[1,128]{1...) custom-call(bf16[256,512]{1,0:T(8,128)(2,1)} %get-tuple-element.23.res_in, ...), custom_call_target="tpu_custom_call" | custom-call | tf_op jit(solution)/shard_map/pallas_call | solution.py:476
